TPU v7x, 512 devices: a whole 4x8x8 slice. The times are simulated.
512 devices in a mesh: dp: 128 (over z, y, core), tensor: 4 (over x).
Axes of the slice: x: 4, y: 8, z: 8, core: 2. Of those that a mesh axis runs over, the one named last changes fastest.
Arguments:
- master: float32 [2, 8192, 2048], P(None, 'dp', 'tensor'), may hold values from -0.0625 to 0.0625
- momentum: float32 [2, 8192, 2048], P(None, 'dp', 'tensor'), may hold values from -6 to 6
- gradient: float32 [2, 8192, 2048], P(None, 'dp', 'tensor'), may hold values from -60 to 60
- bucket_table: int32 [4, 8], P('tensor'), may hold values from 0 to 3, as said below
- tokens: bfloat16 [32768, 8192], P('dp', 'tensor'), may hold values from -6 to 6
- norm_gain: float32 [8192], replicated, may hold values from 0.1 to 1.9
Outputs:
- new_master: float32 [2, 8192, 2048], P(None, 'dp', 'tensor')
- new_momentum: float32 [2, 8192, 2048], P(None, 'dp', 'tensor')
- key_values: bfloat16 [32768, 2048], P('dp', 'tensor')
Inputs may be any that keep to these rules, and one draw needn't show every extreme that they name: `bucket_table`: in each row of 8 entries every value from 0 to 3 appears exactly twice.
All inputs are finite; a program needn't handle non-finite values.
Results may differ from a plain program's by a relative error of at most 0.001.
The roundings to bfloat16 on the way count: a program that leaves them out, or rounds other values in their place, can miss the bound.
Values may be sent and summed in bfloat16 or wider, within the bound.
A program may use at most 128 MiB of HBM per device.

v0:
```python
import math
import jax
import jax.numpy as jnp
from jax import lax
from jax.sharding import Mesh
from jax.sharding import PartitionSpec as P

D = 8192
HD = 128
NS_ITERS = 3
DP = ("dp_0", "dp_1", "dp_2")
beta_momentum = 0.95
learn_rate = 0.05
first_coeff = 3.4445
cube_coeff = -4.775
fifth_coeff = 2.0315
frob_epsilon = 1e-07
rms_epsilon = 1e-05


def rows_for(lines, count):
    spare = -len(lines) % count
    return jnp.pad(lines, [(0, spare)] + [(0, 0)] * (lines.ndim - 1))


def sent_to_all(shard, axis):
    copies = jnp.broadcast_to(shard, (lax.axis_size(axis), *shard.shape))
    return lax.all_to_all(copies, axis, split_axis=0, concat_axis=0, tiled=True)


def joined_along(pieces, dim):
    pieces = jnp.moveaxis(pieces, 0, dim)
    shape = pieces.shape
    return pieces.reshape(*shape[:dim], shape[dim] * shape[dim + 1], *shape[dim + 2 :])


def gathered_by_axis(shard, axes, dim):
    far, near = axes
    pieces = sent_to_all(sent_to_all(shard, far), near)
    return joined_along(pieces.swapaxes(0, 1).reshape(-1, *shard.shape), dim)


def in_blocks(shard, dim, count):
    shape = shard.shape
    pieces = shard.reshape(*shape[:dim], count, shape[dim] // count, *shape[dim + 1 :])
    return jnp.moveaxis(pieces, dim, 0)


def summed_on_arrival(shard, axis, dim):
    count = lax.axis_size(axis)
    pieces = lax.all_to_all(in_blocks(shard, dim, count), axis, 0, 0, tiled=True)
    return jnp.sum(pieces, axis=0)


def sum_by_axis(shard, axes, dim):
    far, near = axes
    pieces = in_blocks(shard, dim, lax.axis_size(far))
    nearer = summed_on_arrival(pieces, near, dim + 1)
    arrived = lax.all_to_all(nearer, far, split_axis=0, concat_axis=0, tiled=True)
    return arrived.sum(axis=0)


def sum_by_parts(shard, axes):
    lines = shard.reshape(-1, shard.shape[-1])
    padded = rows_for(lines, lax.axis_size(axes[0]) * lax.axis_size(axes[1]))
    whole = gathered_by_axis(sum_by_axis(padded, axes, 0), axes, 0)
    return lax.slice_in_dim(whole, 0, len(lines)).reshape(shard.shape)


def to_heads(block, head_size):
    layers = block.shape[0]
    height = block.shape[1]
    slots = block.shape[2] // head_size
    shaped = block.reshape(layers, height, slots, head_size).transpose(0, 2, 1, 3)
    return shaped.reshape(layers * slots, height, head_size)


def from_heads(heads, layers, head_size):
    count = heads.shape[0]
    height = heads.shape[1]
    slots = count // layers
    shaped = heads.reshape(layers, slots, height, head_size).transpose(0, 2, 1, 3)
    return shaped.reshape(layers, height, slots * head_size)


def stack_pairs(heads, order_ids):
    count = heads.shape[0]
    height = heads.shape[1]
    head_size = heads.shape[2]
    picked = jnp.take(heads, order_ids, axis=0)
    picked = picked.reshape(count // 2, 2, height, head_size).transpose(0, 2, 1, 3)
    return picked.reshape(count // 2, height, 2 * head_size)


def unstack_pairs(stacked, order_ids, head_size):
    pairs = stacked.shape[0]
    height = stacked.shape[1]
    split = (
        stacked.reshape(pairs, height, 2, head_size)
        .transpose(0, 2, 1, 3)
        .reshape(2 * pairs, height, head_size)
    )
    inverse = jnp.argsort(order_ids)
    return jnp.take(split, inverse, axis=0)


def local_gram(stacked):
    return jnp.einsum("brk,brj->bkj", stacked, stacked, precision=lax.Precision.HIGHEST)


def polynomial(gram_mat):
    square = jnp.einsum("bkj,bjl->bkl", gram_mat, gram_mat, precision=lax.Precision.HIGHEST)
    return cube_coeff * gram_mat + fifth_coeff * square


def per_device(master, momentum, gradient, bucket_table, tokens, norm_gain):
    new_momentum = beta_momentum * momentum + gradient
    update = gradient + beta_momentum * new_momentum
    layers = master.shape[0]
    heads = to_heads(update, HD)
    count = heads.shape[0]
    sort_keys = bucket_table[0] * count + jnp.arange(count, dtype=jnp.int32)
    order_ids = jnp.argsort(sort_keys)
    stacked = stack_pairs(heads, order_ids)
    width = stacked.shape[2]
    total = sum_by_parts(local_gram(stacked), (("dp_0", "dp_1"), "dp_2"))
    trace_sum = jnp.trace(total, axis1=1, axis2=2)
    scale = 1.0 / (jnp.sqrt(trace_sum) + frob_epsilon)
    gram_mat = total * (scale * scale)[:, None, None]
    identity = jnp.eye(width, dtype=jnp.float32)[None, :, :]
    product = jnp.broadcast_to(identity, gram_mat.shape)
    for iteration in range(NS_ITERS):
        factor = first_coeff * identity + polynomial(gram_mat)
        product = jnp.einsum("bkj,bjl->bkl", product, factor, precision=lax.Precision.HIGHEST)
        if iteration + 1 < NS_ITERS:
            gram_mat = jnp.einsum(
                "bkj,bjl,blm->bkm", factor, gram_mat, factor, precision=lax.Precision.HIGHEST
            )
    current = jnp.einsum(
        "brk,bkj->brj", stacked * scale[:, None, None], product, precision=lax.Precision.HIGHEST
    )
    ortho = from_heads(unstack_pairs(current, order_ids, HD), layers, HD)
    step_scale = learn_rate * math.sqrt(max(1.0, D / (2.0 * HD)))
    new_master = master - step_scale * ortho
    whole = lax.all_gather(tokens, "tensor", axis=1, tiled=True)
    whole_f = whole.astype(jnp.float32)
    sums = jnp.sum(whole_f * whole_f, axis=1)
    normed = (whole_f * lax.rsqrt(sums / D + rms_epsilon)[:, None] * norm_gain[None, :]).astype(
        jnp.bfloat16
    )
    first_weights = new_master[0].astype(jnp.bfloat16)
    projected = jnp.dot(
        normed,
        lax.all_gather(first_weights, DP, axis=0, tiled=True),
        preferred_element_type=jnp.float32,
    )
    return (new_master, new_momentum, projected.astype(jnp.bfloat16))


def solution(mesh):
    torus = Mesh(
        mesh.devices.reshape(8, 8, 2, mesh.shape["tensor"]), ("dp_0", "dp_1", "dp_2", "tensor")
    )
    return jax.shard_map(
        per_device,
        mesh=torus,
        in_specs=(
            P(None, DP, "tensor"),
            P(None, DP, "tensor"),
            P(None, DP, "tensor"),
            P("tensor", None),
            P(DP, "tensor"),
            P(),
        ),
        out_specs=(P(None, DP, "tensor"), P(None, DP, "tensor"), P(DP, "tensor")),
        check_vma=False,
    )
```

profile of v0, /device:TPU:1, one launch (start us, length us, event | category | flops | bytes accessed | tf_op | source)
XLA Modules:
  0.0 200.4 jit_solution(9422798814984269470)
XLA Ops:
  7.8 1.0 sort.31
  8.8 1.8 multiply_add_fusion
  11.8 1.0 fusion.35
  12.9 11.1 %all_to_all.20 = f32[2,64,8,256]{3,2,1,0:T(8,128)S(1)} all-to-all(f32[2,64,8,256]{3,2,1,0:T(8,128)S(1)} %bitcast.49), channel_id=1, replica_groups=mesh['dp_0'=8,'dp_1'=8,'dp_2'=2,'tensor'=4] {'dp_2'}, dimensions={0} | all-to-all | bytes 2097152 | tf_op jit(solution)/shard_map/all_to_all | solution.py:51
  24.0 0.9 reduce_sum.44
  24.9 10.9 %all-to-all-start.1 = ((f32[64,8,256]{2,1,0:T(8,128)}), f32[64,8,256]{2,1,0:T(8,128)S(1)}, u32[]{:S(2)}, u32[]{:S(2)}) async-start(f32[64,8,256]{2,1,0:T(8,128)} %reduce_sum.44), calls=%async_computation.1 | async-start | bytes 1048576 | tf_op jit(solution)/shard_map/all_to_all | solution.py:59
  36.5 16.9 %all-to-all-done.1 = f32[64,8,256]{2,1,0:T(8,128)S(1)} async-done(((f32[64,8,256]{2,1,0:T(8,128)}), f32[64,8,256]{2,1,0:T(8,128)S(1)}, u32[]{:S(2)}, u32[]{:S(2)}) %all-to-all-start.1) | async-done | bytes 524320 | tf_op jit(solution)/shard_map/all_to_all | solution.py:59
  54.3 6.6 %all-to-all-start.2 = ((f32[64,8,256]{2,1,0:T(8,128)}), f32[64,8,256]{2,1,0:T(8,128)S(1)}, u32[]{:S(2)}, u32[]{:S(2)}) async-start(f32[64,8,256]{2,1,0:T(8,128)} %broadcast_in_dim.38), calls=%async_computation.2 | async-start | bytes 1048576 | tf_op jit(solution)/shard_map/all_to_all | solution.py:28
  61.0 1.0 sort.32
  62.1 15.3 %all-to-all-done.2 = f32[64,8,256]{2,1,0:T(8,128)S(1)} async-done(((f32[64,8,256]{2,1,0:T(8,128)}), f32[64,8,256]{2,1,0:T(8,128)S(1)}, u32[]{:S(2)}, u32[]{:S(2)}) %all-to-all-start.2) | async-done | bytes 524320 | tf_op jit(solution)/shard_map/all_to_all | solution.py:28
  77.4 8.4 %all_to_all.21 = f32[2,64,8,256]{3,2,1,0:T(8,128)S(1)} all-to-all(f32[2,64,8,256]{3,2,1,0:T(8,128)S(1)} %broadcast_in_dim.39), channel_id=1, replica_groups=mesh['dp_0'=8,'dp_1'=8,'dp_2'=2,'tensor'=4] {'dp_2'}, dimensions={0} | all-to-all | bytes 2097152 | tf_op jit(solution)/shard_map/all_to_all | solution.py:28
  86.8 1.5 fusion.11
  88.2 1.0 fusion.25
  89.3 1.3 fusion.21
  90.6 1.2 fusion.36
  91.8 1.3 fusion.12
  93.1 1.2 fusion.38
  94.3 1.1 fusion.39
  95.4 1.1 fusion.37
  96.6 1.3 fusion.13
  97.9 1.4 fusion.40
  101.9 3.1 %fusion = f32[256]{0:T(256)S(1)} fusion(bf16[256,8192]{1,0:T(8,128)(2,1)} %all-gather.4.cloned.1.call-done), kind=kLoop, calls=%fused_computation.4 | loop fusion | flops 6291200 | bytes 4195328 | tf_op jit(solution)/shard_map/reduce_sum | solution.py:147
  105.0 80.8 %all-gather.6.cloned.1.call-done = bf16[1,8192,512]{2,1,0:T(8,128)(2,1)} async-done(((bf16[1,64,512]{2,1,0:T(8,128)(2,1)}), bf16[1,8192,512]{2,1,0:T(8,128)(2,1)}) %all-gather.6.cloned.1.call-update) | async-done | bytes 8388624 | tf_op jit(solution)/shard_map/all_gather | solution.py:154
  185.8 7.7 %fusion.14 = bf16[256,512]{1,0:T(8,128)(2,1)} fusion(bf16[1,8192,512]{2,1,0:T(8,128)(2,1)} %all-gather.6.cloned.1.call-done, bf16[256,8192]{1,0:T(8,128)(2,1)} %all-gather.4.cloned.1.call-done, f32[8192]{0:T(1024)S(1)} %copy-done.2, f32[256]{0:T(256)S(1)} %add_rsqrt_fusion), kind=kOutput, calls=%fused_computation.20 | convolution fusion | flops 2156003328 | bytes 12878848 | tf_op jit(solution)/shard_map/dot_general | solution.py:152
  (49 shorter events, 7.2 us)
Async XLA Ops:
  24.9 28.5 %all-to-all-start.1 = ((f32[64,8,256]{2,1,0:T(8,128)}), f32[64,8,256]{2,1,0:T(8,128)S(1)}, u32[]{:S(2)}, u32[]{:S(2)}) async-start(f32[64,8,256]{2,1,0:T(8,128)} %reduce_sum.44), calls=%async_computation.1 | async-start | bytes 1048576 | tf_op jit(solution)/shard_map/all_to_all | solution.py:59
  35.8 66.1 %all-gather.4.cloned.1.call-start = ((), (), s32[]{:S(2)}) async-start(), calls=%async_computation.4 | async-start | bytes 5242880 | tf_op jit(solution)/shard_map/all_gather | solution.py:145
  54.3 23.0 %all-to-all-start.2 = ((f32[64,8,256]{2,1,0:T(8,128)}), f32[64,8,256]{2,1,0:T(8,128)S(1)}, u32[]{:S(2)}, u32[]{:S(2)}) async-start(f32[64,8,256]{2,1,0:T(8,128)} %broadcast_in_dim.38), calls=%async_computation.2 | async-start | bytes 1048576 | tf_op jit(solution)/shard_map/all_to_all | solution.py:28
  60.9 124.9 %all-gather.6.cloned.1.call-start = ((), (), s32[]{:S(2)}) async-start(), calls=%async_computation.5 | async-start | bytes 8454144 | tf_op jit(solution)/shard_map/all_gather | solution.py:154
  94.3 6.8 %copy-start.1 = (f32[2,64,512]{2,1,0:T(8,128)S(1)}, f32[2,64,512]{2,1,0:T(8,128)}, u32[]{:S(2)}) copy-start(f32[2,64,512]{2,1,0:T(8,128)} %param.8) | copy-start | bytes 786436
  96.6 89.2 %copy-start.2 = (f32[8192]{0:T(1024)S(1)}, f32[8192]{0:T(1024)}, u32[]{:S(2)}) copy-start(f32[8192]{0:T(1024)} %param.13) | copy-start | bytes 98308
  101.1 92.4 %copy-start = (f32[2,64,512]{2,1,0:T(8,128)}, f32[2,64,512]{2,1,0:T(8,128)S(1)}, u32[]{:S(2)}) copy-start(f32[2,64,512]{2,1,0:T(8,128)S(1)} %sub.3) | copy-start | bytes 786436
Sparse Core Ops, SparseCore 0:
  38.7 54.2 all-gather.3
  102.0 83.7 all-gather.5
where the time goes:
time: 201 us; the launch traced here: 200 us
  waiting for transfers between devices  114 us (57%)
  matrix products  22 us (11%)
  blocking collectives  19.4 us (10%)
  starting transfers between devices  17.6 us (9%)
  between operations  14.4 us (7%)
  other arithmetic  9.5 us (5%)
  local copies, waits for them, and re-layouts  3.84 us (2%)
    all_gather x1, waiting for transfers between devices, per_device(): lax.all_gather(first_weights, DP, axis=0, tiled=True)  80.8 us
    all_to_all x1, waiting for transfers between devices, sum_by_axis(): lax.all_to_all(nearer, far, split_axis=0, concat_axis=0, tiled=True)  16.9 us
    all_to_all x1, waiting for transfers between devices, sent_to_all(): return lax.all_to_all(copies, axis, split_axis=0, concat_axis=0, tiled=True)  15.3 us
    all_to_all x1, blocking collectives, summed_on_arrival(): lax.all_to_all(in_blocks(shard, dim, count), axis, 0, 0, tiled=True)  11.1 us
    all_to_all x1, starting transfers between devices, sum_by_axis(): lax.all_to_all(nearer, far, split_axis=0, concat_axis=0, tiled=True)  10.9 us
    all_to_all x1, blocking collectives, sent_to_all(): return lax.all_to_all(copies, axis, split_axis=0, concat_axis=0, tiled=True)  8.36 us
    dot_general x1, matrix products, per_device(): jnp.dot(normed, lax.all_gather(first_weights, DP, axis=0, tiled=True), pr...  7.74 us
    all_to_all x1, starting transfers between devices, sent_to_all(): return lax.all_to_all(copies, axis, split_axis=0, concat_axis=0, tiled=True)  6.63 us
  transfers between devices with their start and end apart: 4, of which 3 were waited for; matrix products, arithmetic and copies ran while one was open for 10% of the time, Pallas kernels for 0%

commit v1 on v0

--- a/solution.py
+++ b/solution.py
@@ -151,7 +151,9 @@
     first_weights = new_master[0].astype(jnp.bfloat16)
     projected = jnp.dot(
         normed,
-        lax.all_gather(first_weights, DP, axis=0, tiled=True),
+        jnp.concatenate(
+            lax.all_to_all(jnp.stack([first_weights] * lax.axis_size(DP)), DP, 0, 0), axis=0
+        ),
         preferred_element_type=jnp.float32,
     )
     return (new_master, new_momentum, projected.astype(jnp.bfloat16))

time: 201 us -> 393 us (1.96)
  the two profiles are of different devices: /device:TPU:1 before, /device:TPU:152 now
where the time goes in v1:
time: 393 us
  waiting for transfers between devices  282 us (72%)
  blocking collectives  40.7 us (10%)
  matrix products  22 us (6%)
  starting transfers between devices  17.9 us (5%)
  between operations  14.3 us (4%)
  other arithmetic  8.72 us (2%)
  local copies, waits for them, and re-layouts  7.4 us (2%)
    all_to_all x1, waiting for transfers between devices, per_device(): lax.all_to_all(jnp.stack([first_weights] * lax.axis_size(DP)), DP, 0, 0)  209 us
    all_gather x1, waiting for transfers between devices, per_device(): whole = lax.all_gather(tokens, 'tensor', axis=1, tiled=True)  57 us
    all_to_all x1, blocking collectives, sum_by_axis(): lax.all_to_all(nearer, far, split_axis=0, concat_axis=0, tiled=True)  31.5 us
    all_to_all x1, waiting for transfers between devices, sent_to_all(): return lax.all_to_all(copies, axis, split_axis=0, concat_axis=0, tiled=True)  15.2 us
    all_to_all x1, starting transfers between devices, per_device(): lax.all_to_all(jnp.stack([first_weights] * lax.axis_size(DP)), DP, 0, 0)  10 us
    all_to_all x1, starting transfers between devices, sent_to_all(): return lax.all_to_all(copies, axis, split_axis=0, concat_axis=0, tiled=True)  7.9 us
  transfers between devices with their start and end apart: 3, of which 3 were waited for; matrix products, arithmetic and copies ran while one was open for 1% of the time, Pallas kernels for 0%

profile of v1, /device:TPU:152, one launch (start us, length us, event | category | flops | bytes accessed | tf_op | source)
XLA Modules:
  0.0 392.8 jit_solution(14148730624148931572)
XLA Ops:
  7.8 1.0 sort.31
  8.8 1.8 multiply_add_fusion
  11.8 1.0 fusion.33
  12.9 4.6 %all_to_all.25 = f32[2,64,8,256]{3,2,1,0:T(8,128)S(1)} all-to-all(f32[2,64,8,256]{3,2,1,0:T(8,128)S(1)} %bitcast.48), channel_id=1, replica_groups=mesh['dp_0'=8,'dp_1'=8,'dp_2'=2,'tensor'=4] {'dp_2'}, dimensions={0} | all-to-all | bytes 2097152 | tf_op jit(solution)/shard_map/all_to_all | solution.py:51
  17.6 31.5 %all_to_all.26 = f32[64,8,256]{2,1,0:T(8,128)S(1)} all-to-all(f32[64,8,256]{2,1,0:T(8,128)S(1)} %reduce_sum.44), channel_id=1, replica_groups=mesh['dp_0'=8,'dp_1'=8,'dp_2'=2,'tensor'=4] {'dp_0','dp_1'}, dimensions={0} | all-to-all | bytes 1048576 | tf_op jit(solution)/shard_map/all_to_all | solution.py:59
  50.0 7.9 %all-to-all-start.2 = ((f32[64,8,256]{2,1,0:T(8,128)}), f32[64,8,256]{2,1,0:T(8,128)S(1)}, u32[]{:S(2)}, u32[]{:S(2)}) async-start(f32[64,8,256]{2,1,0:T(8,128)} %broadcast_in_dim.38), calls=%async_computation.2 | async-start | bytes 1048576 | tf_op jit(solution)/shard_map/all_to_all | solution.py:28
  59.0 15.2 %all-to-all-done.2 = f32[64,8,256]{2,1,0:T(8,128)S(1)} async-done(((f32[64,8,256]{2,1,0:T(8,128)}), f32[64,8,256]{2,1,0:T(8,128)S(1)}, u32[]{:S(2)}, u32[]{:S(2)}) %all-to-all-start.2) | async-done | bytes 524320 | tf_op jit(solution)/shard_map/all_to_all | solution.py:28
  74.3 4.6 %all_to_all.27 = f32[2,64,8,256]{3,2,1,0:T(8,128)S(1)} all-to-all(f32[2,64,8,256]{3,2,1,0:T(8,128)S(1)} %broadcast_in_dim.39), channel_id=1, replica_groups=mesh['dp_0'=8,'dp_1'=8,'dp_2'=2,'tensor'=4] {'dp_2'}, dimensions={0} | all-to-all | bytes 2097152 | tf_op jit(solution)/shard_map/all_to_all | solution.py:28
  79.8 1.4 fusion.10
  81.3 1.3 fusion.18
  82.6 1.0 fusion.22
  83.6 1.1 fusion.34
  84.8 1.3 fusion.11
  86.1 1.2 fusion.36
  87.3 1.1 fusion.35
  88.5 1.1 fusion.37
  89.6 1.3 fusion.12
  90.9 1.4 fusion.38
  94.2 4.3 %stack.5 = bf16[128,64,512]{2,1,0:T(8,128)(2,1)} broadcast(bf16[64,512]{1,0:T(8,128)(2,1)S(1)} %fusion.29), dimensions={1,2} | broadcast | bytes 8454144 | tf_op jit(solution)/shard_map/stack | solution.py:155
  98.5 10.0 %all-to-all-start.4 = ((bf16[128,64,512]{2,1,0:T(8,128)(2,1)}), bf16[128,64,512]{2,1,0:T(8,128)(2,1)}, u32[]{:S(2)}, u32[]{:S(2)}) async-start(bf16[128,64,512]{2,1,0:T(8,128)(2,1)} %stack.5), calls=%async_computation.4 | async-start | bytes 16777216 | tf_op jit(solution)/shard_map/all_to_all | solution.py:155
  109.2 57.0 %all-gather.2.cloned.1.call-done = bf16[256,8192]{1,0:T(8,128)(2,1)} async-done(((bf16[256,2048]{1,0:T(8,128)(2,1)}), bf16[256,8192]{1,0:T(8,128)(2,1)}) %all-gather.2.cloned.1.call-update) | async-done | bytes 4194320 | tf_op jit(solution)/shard_map/all_gather | solution.py:145
  166.2 3.1 fusion
  169.3 208.9 %all-to-all-done.4 = bf16[128,64,512]{2,1,0:T(8,128)(2,1)} async-done(((bf16[128,64,512]{2,1,0:T(8,128)(2,1)}), bf16[128,64,512]{2,1,0:T(8,128)(2,1)}, u32[]{:S(2)}, u32[]{:S(2)}) %all-to-all-start.4) | async-done | bytes 8388640 | tf_op jit(solution)/shard_map/all_to_all | solution.py:155
  378.2 7.8 %fusion.13 = bf16[256,512]{1,0:T(8,128)(2,1)} fusion(bf16[8192,512]{1,0:T(8,128)(2,1)} %bitcast.13, bf16[256,8192]{1,0:T(8,128)(2,1)} %all-gather.2.cloned.1.call-done, f32[8192]{0:T(1024)S(1)} %copy-done.2, f32[256]{0:T(256)S(1)} %add_rsqrt_fusion), kind=kOutput, calls=%fused_computation.19 | convolution fusion | flops 2156003328 | bytes 12878848 | tf_op jit(solution)/shard_map/dot_general | solution.py:152
  (48 shorter events, 7.5 us)
Async XLA Ops:
  50.0 24.2 %all-to-all-start.2 = ((f32[64,8,256]{2,1,0:T(8,128)}), f32[64,8,256]{2,1,0:T(8,128)S(1)}, u32[]{:S(2)}, u32[]{:S(2)}) async-start(f32[64,8,256]{2,1,0:T(8,128)} %broadcast_in_dim.38), calls=%async_computation.2 | async-start | bytes 1048576 | tf_op jit(solution)/shard_map/all_to_all | solution.py:28
  87.3 6.8 %copy-start.1 = (f32[2,64,512]{2,1,0:T(8,128)S(1)}, f32[2,64,512]{2,1,0:T(8,128)}, u32[]{:S(2)}) copy-start(f32[2,64,512]{2,1,0:T(8,128)} %param.8) | copy-start | bytes 786436
  94.2 4.3 %copy-start = (f32[2,64,512]{2,1,0:T(8,128)}, f32[2,64,512]{2,1,0:T(8,128)S(1)}, u32[]{:S(2)}) copy-start(f32[2,64,512]{2,1,0:T(8,128)S(1)} %sub.3) | copy-start | bytes 786436
  98.4 279.8 %copy-start.2 = (f32[8192]{0:T(1024)S(1)}, f32[8192]{0:T(1024)}, u32[]{:S(2)}) copy-start(f32[8192]{0:T(1024)} %param.13) | copy-start | bytes 98308
  98.5 279.7 %all-to-all-start.4 = ((bf16[128,64,512]{2,1,0:T(8,128)(2,1)}), bf16[128,64,512]{2,1,0:T(8,128)(2,1)}, u32[]{:S(2)}, u32[]{:S(2)}) async-start(bf16[128,64,512]{2,1,0:T(8,128)(2,1)} %stack.5), calls=%async_computation.4 | async-start | bytes 16777216 | tf_op jit(solution)/shard_map/all_to_all | solution.py:155
  108.5 57.8 %all-gather.2.cloned.1.call-start = ((), (), s32[]{:S(2)}) async-start(), calls=%async_computation.5 | async-start | bytes 5242880 | tf_op jit(solution)/shard_map/all_gather | solution.py:145
Sparse Core Ops, SparseCore 0:
  111.4 54.7 all-gather.1
